TPU v7x, 256 devices: a whole 4x4x8 slice. The times are simulated.
256 devices in a mesh: grp: 16 (over x_hi, y, core), blk: 16 (over x_lo, z).
Axes of the slice: x: 4 (x_hi: 2, x_lo: 2; x = x_hi * 2 + x_lo), y: 4, z: 8, core: 2. Of those that a mesh axis runs over, the one named last changes fastest.
Arguments:
- factors: float32 [1024, 24, 8192], P('grp', None, 'blk'), may hold values from -0.078125 to 0.078125
Outputs:
- exchange_pairs: float32 [9, 512, 16, 512], P(None, 'grp', 'blk')
All inputs are finite; a program needn't handle non-finite values.
Results may differ from a plain program's by a relative error of at most 0.00012.
Values sent between devices are 32-bit elements; how exact they have to be, the bound alone decides.
A program may use at most 256 MiB of HBM per device.

v0:
```python
import jax
import jax.numpy as jnp
from jax import lax
from jax.sharding import PartitionSpec as P


def shifted(block, axis, distance):
    devices = range(lax.axis_size(axis))
    route = [((i - distance) % len(devices), i) for i in devices]
    return lax.ppermute(block, axis, route)


def per_device(factors):
    aux_local, orbitals, block_width = factors.shape
    blk_count = lax.axis_size("blk")
    distances = blk_count // 2 + 1

    def pair_block(visiting):
        return jnp.einsum("pim,pin->mn", visiting, factors, precision=lax.Precision.HIGHEST)

    result = jnp.zeros((distances, block_width, block_width), jnp.float32)
    result = result.at[0].set(pair_block(factors))

    def advance(distance, carry):
        visiting, blocks = carry
        visiting = shifted(visiting, "blk", -1)
        blocks = lax.dynamic_update_index_in_dim(blocks, pair_block(visiting), distance, 0)
        return (visiting, blocks)

    _, result = lax.fori_loop(1, distances, advance, (factors, result))
    result = lax.psum_scatter(result, "grp", scatter_dimension=1, tiled=True)
    return result[:, :, None, :]


def solution(mesh):
    return jax.shard_map(
        per_device,
        mesh=mesh,
        in_specs=(P("grp", None, "blk"),),
        out_specs=P(None, "grp", "blk", None),
        check_vma=False,
    )
```

profile of v0, /device:TPU:8, one launch (start us, length us, event | category | flops | bytes accessed | tf_op | source)
XLA Modules:
  0.0 821.9 jit_solution(4504896110847129865)
XLA Ops:
  6.5 0.0 copy-start
  6.5 0.0 reduce-scatter.2.cloned.1.call-start
  6.5 13.7 %convolution_bitcast_fusion.1 = f32[1,512,512]{2,1,0:T(8,128)} fusion(f32[64,24,512]{2,1,0:T(8,128)} %param.5), kind=kOutput, calls=%fused_computation.2 | convolution fusion | flops 4831838208 | bytes 4194304 | tf_op jit(solution)/shard_map/pim,pin->mn/dot_general | solution.py:19
  20.2 0.0 copy-done
  20.2 3.5 copy.4
  23.7 0.0 copy-start.1
  23.7 4.1 copy.10
  27.8 0.0 copy-done.1
  27.8 4.8 scatter.4
  32.6 666.3 %while.18 = (s32[]{:T(128)}, f32[64,24,512]{2,0,1:T(8,128)}, f32[9,512,512]{2,1,0:T(8,128)}, f32[64,24,512]{2,0,1:T(8,128)}, s32[]{:T(128)}, /*index=5*/s32[]{:T(128)}, s32[]{:T(128)}) while((s32[]{:T(128)}, f32[64,24,512]{2,0,1:T(8,128)}, f32[9,512,512]{2,1,0:T(8,128)}, f32[64,24,512]{2,0,1:T(8,128)}, s32[]{:T(128)}, /*index=5*/s32[]{:T(128)}, ...), condition=%wide.region_1.2_spmd, body=%wide.region_0.0_spmd.sunk | while | flops 4831838208 | bytes 26214552 | solution.py:30
  32.6 6.8 collective-permute-start
  39.4 67.7 %collective-permute-done = f32[64,24,512]{2,0,1:T(8,128)S(1)} collective-permute-done((f32[64,24,512]{2,0,1:T(8,128)}, f32[64,24,512]{2,0,1:T(8,128)S(1)}, u32[]{:S(2)}, u32[]{:S(2)}) %collective-permute-start) | collective-permute-done | bytes 3145760 | tf_op jit(solution)/shard_map/while/body/eval_jaxpr/ppermute | solution.py:10
  107.1 1.6 copy.16
  108.7 12.4 %fusion.10 = f32[9,512,512]{2,1,0:T(8,128)} fusion(f32[9,512,512]{2,1,0:T(8,128)} %get-tuple-element.174, s32[]{:T(128)S(6)} %select_n.12, f32[64,24,512]{2,0,1:T(8,128)S(1)} %collective-permute-done, f32[64,24,512]{2,0,1:T(8,128)} %get-tuple-element.182), kind=kOutput, calls=%fused_computation.1.clone.1 | convolution fusion | flops 4831838208 | bytes 7340036 | tf_op jit(solution)/shard_map/while/body/eval_jaxpr/pim,pin->mn/dot_general | solution.py:19
  121.1 4.5 collective-permute-start
  125.6 66.8 %collective-permute-done = f32[64,24,512]{2,0,1:T(8,128)S(1)} collective-permute-done((f32[64,24,512]{2,0,1:T(8,128)}, f32[64,24,512]{2,0,1:T(8,128)S(1)}, u32[]{:S(2)}, u32[]{:S(2)}) %collective-permute-start) | collective-permute-done | bytes 3145760 | tf_op jit(solution)/shard_map/while/body/eval_jaxpr/ppermute | solution.py:10
  192.4 1.6 copy.16
  194.0 12.4 %fusion.10 = f32[9,512,512]{2,1,0:T(8,128)} fusion(f32[9,512,512]{2,1,0:T(8,128)} %get-tuple-element.174, s32[]{:T(128)S(6)} %select_n.12, f32[64,24,512]{2,0,1:T(8,128)S(1)} %collective-permute-done, f32[64,24,512]{2,0,1:T(8,128)} %get-tuple-element.182), kind=kOutput, calls=%fused_computation.1.clone.1 | convolution fusion | flops 4831838208 | bytes 7340036 | tf_op jit(solution)/shard_map/while/body/eval_jaxpr/pim,pin->mn/dot_general | solution.py:19
  206.4 4.5 collective-permute-start
  210.9 65.9 %collective-permute-done = f32[64,24,512]{2,0,1:T(8,128)S(1)} collective-permute-done((f32[64,24,512]{2,0,1:T(8,128)}, f32[64,24,512]{2,0,1:T(8,128)S(1)}, u32[]{:S(2)}, u32[]{:S(2)}) %collective-permute-start) | collective-permute-done | bytes 3145760 | tf_op jit(solution)/shard_map/while/body/eval_jaxpr/ppermute | solution.py:10
  276.8 1.6 copy.16
  278.4 12.4 %fusion.10 = f32[9,512,512]{2,1,0:T(8,128)} fusion(f32[9,512,512]{2,1,0:T(8,128)} %get-tuple-element.174, s32[]{:T(128)S(6)} %select_n.12, f32[64,24,512]{2,0,1:T(8,128)S(1)} %collective-permute-done, f32[64,24,512]{2,0,1:T(8,128)} %get-tuple-element.182), kind=kOutput, calls=%fused_computation.1.clone.1 | convolution fusion | flops 4831838208 | bytes 7340036 | tf_op jit(solution)/shard_map/while/body/eval_jaxpr/pim,pin->mn/dot_general | solution.py:19
  290.8 4.5 collective-permute-start
  295.3 65.0 %collective-permute-done = f32[64,24,512]{2,0,1:T(8,128)S(1)} collective-permute-done((f32[64,24,512]{2,0,1:T(8,128)}, f32[64,24,512]{2,0,1:T(8,128)S(1)}, u32[]{:S(2)}, u32[]{:S(2)}) %collective-permute-start) | collective-permute-done | bytes 3145760 | tf_op jit(solution)/shard_map/while/body/eval_jaxpr/ppermute | solution.py:10
  360.2 1.6 copy.16
  361.9 12.4 %fusion.10 = f32[9,512,512]{2,1,0:T(8,128)} fusion(f32[9,512,512]{2,1,0:T(8,128)} %get-tuple-element.174, s32[]{:T(128)S(6)} %select_n.12, f32[64,24,512]{2,0,1:T(8,128)S(1)} %collective-permute-done, f32[64,24,512]{2,0,1:T(8,128)} %get-tuple-element.182), kind=kOutput, calls=%fused_computation.1.clone.1 | convolution fusion | flops 4831838208 | bytes 7340036 | tf_op jit(solution)/shard_map/while/body/eval_jaxpr/pim,pin->mn/dot_general | solution.py:19
  374.3 4.5 collective-permute-start
  378.8 64.0 %collective-permute-done = f32[64,24,512]{2,0,1:T(8,128)S(1)} collective-permute-done((f32[64,24,512]{2,0,1:T(8,128)}, f32[64,24,512]{2,0,1:T(8,128)S(1)}, u32[]{:S(2)}, u32[]{:S(2)}) %collective-permute-start) | collective-permute-done | bytes 3145760 | tf_op jit(solution)/shard_map/while/body/eval_jaxpr/ppermute | solution.py:10
  442.8 1.6 copy.16
  444.4 12.4 %fusion.10 = f32[9,512,512]{2,1,0:T(8,128)} fusion(f32[9,512,512]{2,1,0:T(8,128)} %get-tuple-element.174, s32[]{:T(128)S(6)} %select_n.12, f32[64,24,512]{2,0,1:T(8,128)S(1)} %collective-permute-done, f32[64,24,512]{2,0,1:T(8,128)} %get-tuple-element.182), kind=kOutput, calls=%fused_computation.1.clone.1 | convolution fusion | flops 4831838208 | bytes 7340036 | tf_op jit(solution)/shard_map/while/body/eval_jaxpr/pim,pin->mn/dot_general | solution.py:19
  456.8 4.5 collective-permute-start
  461.3 63.1 %collective-permute-done = f32[64,24,512]{2,0,1:T(8,128)S(1)} collective-permute-done((f32[64,24,512]{2,0,1:T(8,128)}, f32[64,24,512]{2,0,1:T(8,128)S(1)}, u32[]{:S(2)}, u32[]{:S(2)}) %collective-permute-start) | collective-permute-done | bytes 3145760 | tf_op jit(solution)/shard_map/while/body/eval_jaxpr/ppermute | solution.py:10
  524.4 1.6 copy.16
  526.1 12.4 %fusion.10 = f32[9,512,512]{2,1,0:T(8,128)} fusion(f32[9,512,512]{2,1,0:T(8,128)} %get-tuple-element.174, s32[]{:T(128)S(6)} %select_n.12, f32[64,24,512]{2,0,1:T(8,128)S(1)} %collective-permute-done, f32[64,24,512]{2,0,1:T(8,128)} %get-tuple-element.182), kind=kOutput, calls=%fused_computation.1.clone.1 | convolution fusion | flops 4831838208 | bytes 7340036 | tf_op jit(solution)/shard_map/while/body/eval_jaxpr/pim,pin->mn/dot_general | solution.py:19
  538.5 4.5 collective-permute-start
  543.0 62.2 %collective-permute-done = f32[64,24,512]{2,0,1:T(8,128)S(1)} collective-permute-done((f32[64,24,512]{2,0,1:T(8,128)}, f32[64,24,512]{2,0,1:T(8,128)S(1)}, u32[]{:S(2)}, u32[]{:S(2)}) %collective-permute-start) | collective-permute-done | bytes 3145760 | tf_op jit(solution)/shard_map/while/body/eval_jaxpr/ppermute | solution.py:10
  605.1 1.6 copy.16
  606.8 12.4 %fusion.10 = f32[9,512,512]{2,1,0:T(8,128)} fusion(f32[9,512,512]{2,1,0:T(8,128)} %get-tuple-element.174, s32[]{:T(128)S(6)} %select_n.12, f32[64,24,512]{2,0,1:T(8,128)S(1)} %collective-permute-done, f32[64,24,512]{2,0,1:T(8,128)} %get-tuple-element.182), kind=kOutput, calls=%fused_computation.1.clone.1 | convolution fusion | flops 4831838208 | bytes 7340036 | tf_op jit(solution)/shard_map/while/body/eval_jaxpr/pim,pin->mn/dot_general | solution.py:19
  619.2 4.5 collective-permute-start
  623.7 61.3 %collective-permute-done = f32[64,24,512]{2,0,1:T(8,128)S(1)} collective-permute-done((f32[64,24,512]{2,0,1:T(8,128)}, f32[64,24,512]{2,0,1:T(8,128)S(1)}, u32[]{:S(2)}, u32[]{:S(2)}) %collective-permute-start) | collective-permute-done | bytes 3145760 | tf_op jit(solution)/shard_map/while/body/eval_jaxpr/ppermute | solution.py:10
  684.9 1.6 copy.16
  686.6 12.4 %fusion.10 = f32[9,512,512]{2,1,0:T(8,128)} fusion(f32[9,512,512]{2,1,0:T(8,128)} %get-tuple-element.174, s32[]{:T(128)S(6)} %select_n.12, f32[64,24,512]{2,0,1:T(8,128)S(1)} %collective-permute-done, f32[64,24,512]{2,0,1:T(8,128)} %get-tuple-element.182), kind=kOutput, calls=%fused_computation.1.clone.1 | convolution fusion | flops 4831838208 | bytes 7340036 | tf_op jit(solution)/shard_map/while/body/eval_jaxpr/pim,pin->mn/dot_general | solution.py:19
  699.0 0.0 reduce-scatter.2.cloned.1.call-update
  699.0 113.8 %reduce-scatter.2.cloned.1.call-done = f32[9,32,512]{2,1,0:T(8,128)} async-done(((f32[9,512,512]{2,1,0:T(8,128)}), f32[9,32,512]{2,1,0:T(8,128)}) %reduce-scatter.2.cloned.1.call-update) | async-done | bytes 589840 | tf_op jit(solution)/shard_map/reduce_scatter | solution.py:31
  812.8 2.3 broadcast_in_dim.15
Async XLA Ops:
  6.5 13.7 %copy-start = (f32[64,24,512]{2,1,0:T(8,128)S(1)}, f32[64,24,512]{2,1,0:T(8,128)}, u32[]{:S(2)}) copy-start(f32[64,24,512]{2,1,0:T(8,128)} %param.5) | copy-start | bytes 9437188
  6.5 806.2 %reduce-scatter.2.cloned.1.call-start = ((), (), s32[]{:S(2)}) async-start(), calls=%async_computation.1 | async-start | bytes 10027008 | tf_op jit(solution)/shard_map/reduce_scatter | solution.py:31
  23.7 4.1 copy-start.1
  32.6 74.5 %collective-permute-start = (f32[64,24,512]{2,0,1:T(8,128)}, f32[64,24,512]{2,0,1:T(8,128)S(1)}, u32[]{:S(2)}, u32[]{:S(2)}) collective-permute-start(f32[64,24,512]{2,0,1:T(8,128)} %get-tuple-element.173), channel_id=1, source_target_pairs={{1,0},{2,1},{3,2},{4,3},{5,4},{6,5},{7,6},{8,7},{9,8},{10,9},{11,1... | collective-permute-start | bytes 9437192 | tf_op jit(solution)/shard_map/while/body/eval_jaxpr/ppermute | solution.py:10
  121.1 71.3 %collective-permute-start = (f32[64,24,512]{2,0,1:T(8,128)}, f32[64,24,512]{2,0,1:T(8,128)S(1)}, u32[]{:S(2)}, u32[]{:S(2)}) collective-permute-start(f32[64,24,512]{2,0,1:T(8,128)} %get-tuple-element.173), channel_id=1, source_target_pairs={{1,0},{2,1},{3,2},{4,3},{5,4},{6,5},{7,6},{8,7},{9,8},{10,9},{11,1... | collective-permute-start | bytes 9437192 | tf_op jit(solution)/shard_map/while/body/eval_jaxpr/ppermute | solution.py:10
  206.4 70.4 %collective-permute-start = (f32[64,24,512]{2,0,1:T(8,128)}, f32[64,24,512]{2,0,1:T(8,128)S(1)}, u32[]{:S(2)}, u32[]{:S(2)}) collective-permute-start(f32[64,24,512]{2,0,1:T(8,128)} %get-tuple-element.173), channel_id=1, source_target_pairs={{1,0},{2,1},{3,2},{4,3},{5,4},{6,5},{7,6},{8,7},{9,8},{10,9},{11,1... | collective-permute-start | bytes 9437192 | tf_op jit(solution)/shard_map/while/body/eval_jaxpr/ppermute | solution.py:10
  290.8 69.4 %collective-permute-start = (f32[64,24,512]{2,0,1:T(8,128)}, f32[64,24,512]{2,0,1:T(8,128)S(1)}, u32[]{:S(2)}, u32[]{:S(2)}) collective-permute-start(f32[64,24,512]{2,0,1:T(8,128)} %get-tuple-element.173), channel_id=1, source_target_pairs={{1,0},{2,1},{3,2},{4,3},{5,4},{6,5},{7,6},{8,7},{9,8},{10,9},{11,1... | collective-permute-start | bytes 9437192 | tf_op jit(solution)/shard_map/while/body/eval_jaxpr/ppermute | solution.py:10
  374.3 68.5 %collective-permute-start = (f32[64,24,512]{2,0,1:T(8,128)}, f32[64,24,512]{2,0,1:T(8,128)S(1)}, u32[]{:S(2)}, u32[]{:S(2)}) collective-permute-start(f32[64,24,512]{2,0,1:T(8,128)} %get-tuple-element.173), channel_id=1, source_target_pairs={{1,0},{2,1},{3,2},{4,3},{5,4},{6,5},{7,6},{8,7},{9,8},{10,9},{11,1... | collective-permute-start | bytes 9437192 | tf_op jit(solution)/shard_map/while/body/eval_jaxpr/ppermute | solution.py:10
  456.8 67.6 %collective-permute-start = (f32[64,24,512]{2,0,1:T(8,128)}, f32[64,24,512]{2,0,1:T(8,128)S(1)}, u32[]{:S(2)}, u32[]{:S(2)}) collective-permute-start(f32[64,24,512]{2,0,1:T(8,128)} %get-tuple-element.173), channel_id=1, source_target_pairs={{1,0},{2,1},{3,2},{4,3},{5,4},{6,5},{7,6},{8,7},{9,8},{10,9},{11,1... | collective-permute-start | bytes 9437192 | tf_op jit(solution)/shard_map/while/body/eval_jaxpr/ppermute | solution.py:10
  538.5 66.7 %collective-permute-start = (f32[64,24,512]{2,0,1:T(8,128)}, f32[64,24,512]{2,0,1:T(8,128)S(1)}, u32[]{:S(2)}, u32[]{:S(2)}) collective-permute-start(f32[64,24,512]{2,0,1:T(8,128)} %get-tuple-element.173), channel_id=1, source_target_pairs={{1,0},{2,1},{3,2},{4,3},{5,4},{6,5},{7,6},{8,7},{9,8},{10,9},{11,1... | collective-permute-start | bytes 9437192 | tf_op jit(solution)/shard_map/while/body/eval_jaxpr/ppermute | solution.py:10
  619.2 65.8 %collective-permute-start = (f32[64,24,512]{2,0,1:T(8,128)}, f32[64,24,512]{2,0,1:T(8,128)S(1)}, u32[]{:S(2)}, u32[]{:S(2)}) collective-permute-start(f32[64,24,512]{2,0,1:T(8,128)} %get-tuple-element.173), channel_id=1, source_target_pairs={{1,0},{2,1},{3,2},{4,3},{5,4},{6,5},{7,6},{8,7},{9,8},{10,9},{11,1... | collective-permute-start | bytes 9437192 | tf_op jit(solution)/shard_map/while/body/eval_jaxpr/ppermute | solution.py:10
Sparse Core Ops, SparseCore 0:
  699.1 113.5 reduce-scatter.1
where the time goes:
time: 822 us
  waiting for transfers between devices  630 us (77%)
  matrix products  113 us (14%)
  starting transfers between devices  38.2 us (5%)
  local copies, waits for them, and re-layouts  27.8 us (3%)
  between operations  13.4 us (2%)
    ppermute x8, waiting for transfers between devices, shifted(): return lax.ppermute(block, axis, route)  516 us
    reduce_scatter x1, waiting for transfers between devices, per_device(): result = lax.psum_scatter(result, 'grp', scatter_dimension=1, tiled=True)  114 us
    dot_general x9, matrix products, pair_block(): jnp.einsum('pim,pin->mn', visiting, factors, precision=lax.Precision.HIGH...  113 us
    ppermute x8, starting transfers between devices, shifted(): return lax.ppermute(block, axis, route)  38.2 us
  transfers between devices with their start and end apart: 9, of which 9 were waited for; matrix products, arithmetic and copies ran while one was open for 0% of the time, Pallas kernels for 0%

commit v1 on v0

v1 whole, which is shorter than its diff:
```python
import jax
import jax.numpy as jnp
from jax import lax
from jax.experimental import pallas as pl
from jax.experimental.pallas import tpu as pltpu
from jax.sharding import PartitionSpec as P

MESH = pl.DeviceIdType.MESH
OWN, P1, M1, Q1, M2, P2, Q2 = range(7)
OFFSET = {OWN: (0, 0), P1: (0, 1), M1: (0, -1), Q1: (1, 1), M2: (0, -2), P2: (0, 2), Q2: (1, 2)}
PAIRS = [(OWN, OWN), (P1, OWN), (P1, M1), (Q1, P1), (Q1, OWN), (Q1, M1), (M2, P1), (M2, Q1), (M2, P2), (M2, Q2)]
BATCHES = [(0, 12), (12, 12), (24, 6), (30, 10)]
TILES = 40


def kernel(x, out, f32, q2, own, hi, lo, prod, core_in, y_in, fin,
           link_send, link_recv, own_sem, core_send, core_recv, y_send, y_recv, fin_send, fin_recv):
    grp, blk = lax.axis_index("grp"), lax.axis_index("blk")
    core, y, h = lax.rem(grp, 2), lax.rem(lax.div(grp, 2), 4), lax.div(grp, 8)
    z, row = lax.rem(blk, 8), lax.div(blk, 8)
    part = f32.shape[2] // 2

    def at_blk(dl, dz):
        return lax.rem(row + dl, 2) * 8 + lax.rem(z + dz + 8, 8)

    def at_grp(dh, dy, dk):
        return lax.rem(h + dh, 2) * 8 + lax.rem(y + dy, 4) * 2 + lax.rem(core + dk, 2)

    greet = [(grp, at_blk(1, 0)), (at_grp(0, 0, 1), blk)]
    greet += [(at_grp(0, dy, 0), blk) for dy in (1, 2, 3)]
    plane = [(0, 0), (0, 1), (0, -1), (0, 2), (0, -2), (1, 1), (1, -1), (1, 2), (1, -2)]
    for dh in range(2):
        greet += [(at_grp(dh, 0, 0), at_blk(dl, dz)) for dl, dz in plane if (dh, dl, dz) != (0, 0, 0)]
    barrier = pltpu.get_barrier_semaphore()
    for dev in greet:
        pl.semaphore_signal(barrier, inc=1, device_id=dev, device_id_type=MESH)
    pl.semaphore_wait(barrier, len(greet))

    down, up, across = (grp, at_blk(0, -1)), (grp, at_blk(0, 1)), (grp, at_blk(1, 0))

    def half_of(step):
        return lax.rem(1 - row + step, 2)

    def window(buf, half, step):
        return buf.at[half, pl.ds(half_of(step) * part, part)]

    def link(stream, half, step):
        slot = (P1, M1, P2, M2, Q1, Q2)[stream]
        dev = (down, up, down, up, across, across)[stream]
        sem = stream * 4 + half * 2 + step
        if stream < 2:
            src = x.at[pl.ds(half_of(step) * part, part), :, pl.ds(half * 256, 256)]
        else:
            src = window(f32.at[(P1, M1, P1, P2)[stream - 2] - 1], half, step)
        dst = q2.at[half] if slot == Q2 else window(f32.at[slot - 1], half, step)
        return pltpu.make_async_remote_copy(src_ref=src, dst_ref=dst, send_sem=link_send.at[sem],
                                            recv_sem=link_recv.at[sem], device_id=dev, device_id_type=MESH)

    pieces = [(half, step) for half in range(2) for step in range(2)]
    for half, step in pieces:
        link(0, half, step).start()
        link(1, half, step).start()

    def split(a, slot, half, kh):
        a = a.reshape(-1, 256)
        top = a.astype(jnp.bfloat16)
        hi[slot, half, kh] = top
        lo[slot, half, kh] = (a - top.astype(jnp.float32)).astype(jnp.bfloat16)

    def split_slot(slot, half):
        @pl.loop(0, 2)
        def _(kh):
            split(f32[slot - 1, half, pl.ds(kh * part, part)], slot, half, kh)

    @pl.loop(0, 4)
    def _(i):
        half, kh = lax.div(i, 2), lax.rem(i, 2)
        copy = pltpu.make_async_copy(
            x.at[pl.ds(kh * part, part), :, pl.ds(pl.multiple_of(half * 256, 256), 256)], own, own_sem)
        copy.start()
        copy.wait()
        split(own[...], OWN, half, kh)

    meta = []
    for s, t in PAIRS:
        i, j = at_blk(*OFFSET[s]), at_blk(*OFFSET[t])
        diff = lax.rem(i - j + 16, 16)
        straight = diff <= 8
        meta.append((straight, jnp.where(straight, s, t), jnp.where(straight, t, s),
                     jnp.where(straight, j, i), jnp.where(straight, diff, 16 - diff)))
    share = {8: lax.div(z, 4), 9: row}

    def tile(pair, a, b, pos):
        _, rows, cols, _, _ = meta[pair]
        dims = (((0,), (0,)), ((), ()))
        total = None
        for kh in ([share[pair]] if pair in share else [0, 1]):
            for left, right in ((hi, hi), (hi, lo), (lo, hi)):
                term = lax.dot_general(left[rows, a, kh], right[cols, b, kh], dims,
                                       preferred_element_type=jnp.float32)
                total = term if total is None else total + term
        total = total.reshape(4, 2, 32, 256)
        prod[0, pos] = total[:, 0]
        prod[1, pos] = total[:, 1]

    def place(pair, i, j):
        straight = meta[pair][0]
        return jnp.where(straight, i, j), jnp.where(straight, j, i)

    def whole_pair(pair):
        @pl.loop(0, 4)
        def _(q):
            tile(pair, lax.div(q, 2), lax.rem(q, 2), pair * 4 + q)

    def late(pair, half):
        if pair < 8:
            return 2, lambda t: (half, t)
        if half == 0:
            return 1, lambda t: (0, 0)
        return 3, lambda t: (lax.div(t + 1, 2), lax.rem(t + 1, 2))

    first = {}
    pos = 24
    for half in range(2):
        for pair in (6, 7, 8, 9):
            first[pair, half] = pos
            pos += late(pair, half)[0]

    def late_pair(pair, half):
        count, halves = late(pair, half)

        @pl.loop(0, count)
        def _(t):
            a, b = place(pair, *halves(t))
            tile(pair, a, b, first[pair, half] + t)

    def core_copy(batch):
        start, n = BATCHES[batch]
        return pltpu.make_async_remote_copy(
            src_ref=prod.at[1 - core, pl.ds(start, n)], dst_ref=core_in.at[pl.ds(start, n)],
            send_sem=core_send.at[batch], recv_sem=core_recv.at[batch],
            device_id=(at_grp(0, 0, 1), blk), device_id_type=MESH)

    def y_copy(batch, dy):
        start, n = BATCHES[batch]
        return pltpu.make_async_remote_copy(
            src_ref=prod.at[core, pl.ds(start, n), lax.rem(y + dy, 4)], dst_ref=y_in.at[dy - 1, pl.ds(start, n)],
            send_sem=y_send.at[batch * 3 + dy - 1], recv_sem=y_recv.at[batch * 3 + dy - 1],
            device_id=(at_grp(0, dy, 0), blk), device_id_type=MESH)

    def core_finish(batch):
        start, n = BATCHES[batch]
        core_copy(batch).wait()

        @pl.loop(start, start + n)
        def _(q):
            prod[core, q] = prod[core, q] + core_in[q]

        for dy in (1, 2, 3):
            y_copy(batch, dy).start()

    def fin_copy(pair, a, b, pos, wait):
        _, _, _, owner, distance = meta[pair]
        slot = distance + 5 * share[pair] if pair in share else distance
        mine = jnp.logical_and(a == h, owner == blk)
        src, dst, sem = prod.at[core, pos, y], fin.at[slot, h, b], fin_recv.at[slot * 4 + h * 2 + b]
        if not wait:
            @pl.when(mine)
            def _():
                pltpu.make_async_copy(src, dst, sem).start()

        @pl.when(jnp.logical_not(mine))
        def _():
            copy = pltpu.make_async_remote_copy(
                src_ref=src, dst_ref=dst, send_sem=fin_send.at[pos], recv_sem=sem,
                device_id=(a * 8 + y * 2 + core, owner), device_id_type=MESH)
            if wait:
                copy.wait_send()
            else:
                copy.start()

    def fin_batch(batch, wait):
        if batch < 2:
            for pair in range(3 * batch, 3 * batch + 3):
                @pl.loop(0, 4)
                def _(q, pair=pair):
                    fin_copy(pair, lax.div(q, 2), lax.rem(q, 2), pair * 4 + q, wait)
        else:
            for pair in (6, 7, 8, 9):
                count, halves = late(pair, batch - 2)

                @pl.loop(0, count)
                def _(t, pair=pair, halves=halves):
                    a, b = place(pair, *halves(t))
                    fin_copy(pair, a, b, first[pair, batch - 2] + t, wait)

    def y_finish(batch):
        start, n = BATCHES[batch]
        for dy in (1, 2, 3):
            y_copy(batch, dy).wait()

        @pl.loop(start, start + n)
        def _(q):
            prod[core, q, y] = (prod[core, q, y] + y_in[0, q]) + (y_in[1, q] + y_in[2, q])

        fin_batch(batch, False)

    whole_pair(0)
    for half, step in pieces:
        link(0, half, step).wait_recv()
        link(2, half, step).start()
        link(4, half, step).start()
        link(1, half, step).wait_recv()
        link(3, half, step).start()
    for half in range(2):
        split_slot(P1, half)
        split_slot(M1, half)
    whole_pair(1)
    whole_pair(2)
    core_copy(0).start()
    for half, step in pieces:
        link(4, half, step).wait_recv()
    link(2, 0, 0).wait_recv()
    link(5, 0, 0).start()
    for half in range(2):
        split_slot(Q1, half)
    for pair in (3, 4, 5):
        whole_pair(pair)
    core_copy(1).start()
    core_finish(0)
    core_finish(1)
    y_finish(0)

    for half in range(2):
        if half == 1:
            link(2, 1, 0).wait_recv()
            link(5, 1, 0).start()
            core_finish(2)
            y_finish(1)
        link(3, half, 0).wait_recv()
        link(3, half, 1).wait_recv()
        split_slot(M2, half)
        late_pair(6, half)
        late_pair(7, half)
        if half == 1:
            y_finish(2)
        link(2, half, 1).wait_recv()
        split_slot(P2, half)
        late_pair(8, half)
        link(5, half, 0).wait_recv()
        split(q2[half], Q2, half, row)
        late_pair(9, half)
        core_copy(2 + half).start()
    core_finish(3)
    y_finish(3)

    for d in [0, 1, 2, 3, 5, 6, 7, 8, 4]:
        slots = [d, 9] if d == 4 else [d]
        for b in range(2):
            for slot in slots:
                for src in range(2):
                    pltpu.make_async_copy(fin.at[slot, src, b], fin.at[slot, src, b],
                                          fin_recv.at[slot * 4 + src * 2 + b]).wait()
            total = fin[d, 0, b] + fin[d, 1, b]
            if d == 4:
                total = total + (fin[9, 0, b] + fin[9, 1, b])
            out[d, :, b * 256:(b + 1) * 256] = total

    for half, step in pieces:
        for stream in range(6 if step == 0 else 5):
            link(stream, half, step).wait_send()
    for batch in range(4):
        fin_batch(batch, True)


def per_device(factors):
    aux, orbitals, width = factors.shape
    part = aux // 2
    depth = part * orbitals
    dma = pltpu.SemaphoreType.DMA
    out = pl.pallas_call(
        kernel,
        out_shape=jax.ShapeDtypeStruct((9, 32, width), jnp.float32),
        in_specs=[pl.BlockSpec(memory_space=pl.ANY)],
        out_specs=pl.BlockSpec(memory_space=pltpu.VMEM),
        scratch_shapes=[
            pltpu.VMEM((5, 2, aux, orbitals, 256), jnp.float32),
            pltpu.VMEM((2, part, orbitals, 256), jnp.float32),
            pltpu.VMEM((part, orbitals, 256), jnp.float32),
            pltpu.VMEM((7, 2, 2, depth, 256), jnp.bfloat16),
            pltpu.VMEM((7, 2, 2, depth, 256), jnp.bfloat16),
            pltpu.VMEM((2, TILES, 4, 32, 256), jnp.float32),
            pltpu.VMEM((TILES, 4, 32, 256), jnp.float32),
            pltpu.VMEM((3, TILES, 32, 256), jnp.float32),
            pltpu.VMEM((10, 2, 2, 32, 256), jnp.float32),
            dma((24,)), dma((24,)), dma, dma((4,)), dma((4,)), dma((12,)), dma((12,)), dma((TILES,)), dma((40,)),
        ],
        compiler_params=pltpu.CompilerParams(
            collective_id=0, has_side_effects=True, vmem_limit_bytes=62 * 2**20),
        cost_estimate=pl.CostEstimate(flops=6 * 9 * 512 * 512 * aux * orbitals, bytes_accessed=4 * 2**20,
                                      transcendentals=0),
        name="exchange",
    )(factors)
    return out[:, :, None, :]


def solution(mesh):
    return jax.shard_map(
        per_device,
        mesh=mesh,
        in_specs=(P("grp", None, "blk"),),
        out_specs=P(None, "grp", "blk", None),
        check_vma=False,
    )
```

time: 822 us -> 196 us (0.24)
  waiting for transfers between devices: 630 us -> 0 us
  Pallas kernels: 0 us -> 191 us
  matrix products: 113 us -> 0 us
  starting transfers between devices: 38.2 us -> 0 us
  local copies, waits for them, and re-layouts: 27.8 us -> 2.49 us
  between operations: 13.4 us -> 0.01 us
    ppermute x8 -> x0, waiting for transfers between devices: 516 us -> none  [shifted(): return lax.ppermute(block, axis, route)]
    pallas_call x0 -> x1, Pallas kernels: none -> 191 us  [per_device(): pl.pallas_call(kernel, out_shape=jax.ShapeDtypeStruct((9, 32, width), jnp...]
    reduce_scatter x1 -> x0, waiting for transfers between devices: 114 us -> none  [per_device(): result = lax.psum_scatter(result, 'grp', scatter_dimension=1, tiled=True)]
    dot_general x9 -> x0, matrix products: 113 us -> none  [pair_block(): jnp.einsum('pim,pin->mn', visiting, factors, precision=lax.Precision.HIGH...]
    ppermute x8 -> x0, starting transfers between devices: 38.2 us -> none  [shifted(): return lax.ppermute(block, axis, route)]
    while x9 -> x0, local copies, waits for them, and re-layouts: 16.6 us -> none
  transfers between devices with their start and end apart: 9 -> 0, of which waited for: 9 -> 0; matrix products, arithmetic and copies ran while one was open for 0% -> 0% of each run, Pallas kernels for 0% -> 0%
where the time goes in v1:
time: 196 us; the launch traced here: 193 us
  Pallas kernels  191 us (97%)
  local copies, waits for them, and re-layouts  2.49 us (1%)
    pallas_call x1, Pallas kernels, per_device(): pl.pallas_call(kernel, out_shape=jax.ShapeDtypeStruct((9, 32, width), jnp...  191 us

profile of v1, /device:TPU:8, one launch (start us, length us, event | category | flops | bytes accessed | tf_op | source)
XLA Modules:
  0.0 193.4 jit_solution(5133510544873094662)
XLA Ops:
  0.0 190.9 %exchange.1 = f32[9,32,512]{2,1,0:T(8,128)} custom-call(f32[64,24,512]{2,1,0:T(8,128)} %x.1), custom_call_target="tpu_custom_call" | custom-call | flops 21743271936 | bytes 4194304 | tf_op jit(solution)/shard_map/exchange/pallas_call | solution.py:281
  190.9 2.5 %copy.2 = f32[9,32,1,512]{3,2,1,0:T(1,128)} copy(f32[9,32,1,512]{3,1,0,2:T(8,128)} %bitcast.1) | data formatting | bytes 1179648 | tf_op jit(solution)/shard_map/broadcast_in_dim | solution.py:304

commit v2 on v0

v2 whole, which is shorter than its diff:
```python
import jax
import jax.numpy as jnp
from jax import lax
from jax.experimental import pallas as pl
from jax.experimental.pallas import tpu as pltpu
from jax.sharding import PartitionSpec as P

MESH = pl.DeviceIdType.MESH
OWN, P1, M1, Q1, M2, P2, Q2 = range(7)
OFFSET = [(0, 0), (0, 1), (0, -1), (1, 1), (0, -2), (0, 2), (1, 2)]
ORDER = [0, 3, 5, 2, 7, 1, 4, 6]
N_M2, N_P2 = 5, 4


def pairs(s, t, halves):
    return [(s, i, t, j) for i, j in halves]


ALL = [(0, 0), (0, 1), (1, 0), (1, 1)]
A, B = [(0, 0), (0, 1)], [(1, 0), (1, 1)]
BATCHES = [
    [(8, pairs(OWN, OWN, ALL))],
    [(8, pairs(P1, OWN, A) + pairs(P1, M1, ALL[:1])), (8, pairs(Q1, OWN, A) + pairs(Q1, P1, ALL[:1]) + pairs(Q1, M1, ALL[:1]))],
    [(8, pairs(P1, OWN, B) + pairs(P1, M1, ALL[1:]) + pairs(Q1, P1, ALL[1:2]) + pairs(Q1, M1, ALL[1:2]))],
    [(8, pairs(Q1, OWN, B) + pairs(Q1, P1, B) + pairs(Q1, M1, B))],
    [(5, pairs(M2, P1, A) + pairs(M2, Q1, A)), (3, pairs(P2, M1, A) + pairs(Q2, M1, A)),
     (4, pairs(M2, P2, ALL[:1]) + pairs(M2, Q2, ALL[:1]))],
    [(3, pairs(P2, M1, B) + pairs(Q2, M1, B)), (4, pairs(M2, P2, ALL[1:2]) + pairs(M2, Q2, ALL[1:2]))],
    [(5, pairs(M2, P1, B) + pairs(M2, Q1, B)), (4, pairs(M2, P2, B) + pairs(M2, Q2, B))],
]
FIRST, COUNT = [], []
for batch in BATCHES:
    FIRST.append(sum(COUNT))
    COUNT.append(sum(len(tiles) for _, tiles in batch))
TILES = sum(COUNT)


def pick(t, values):
    out = values[0]
    for k in range(1, len(values)):
        if values[k] != values[k - 1]:
            out = jnp.where(t >= k, values[k], out)
    return out


def kernel(x, out, near, m2, p2, q2, own, hi, lo, prod, core_in, y_in, fin,
           link_send, link_recv, own_sem, core_send, core_recv, y_send, y_recv, fin_send, fin_recv):
    grp, blk = lax.axis_index("grp"), lax.axis_index("blk")
    core, y, h = lax.rem(grp, 2), lax.rem(lax.div(grp, 2), 4), lax.div(grp, 8)
    z, row = lax.rem(blk, 8), lax.div(blk, 8)
    chunk = near.shape[2] // 8
    piece = near.shape[2] // 4

    def at_blk(dl, dz):
        return lax.rem(row + dl, 2) * 8 + lax.rem(z + dz + 8, 8)

    def at_grp(dh, dy, dk):
        return lax.rem(h + dh, 2) * 8 + lax.rem(y + dy, 4) * 2 + lax.rem(core + dk, 2)

    greet = [(grp, at_blk(1, 0)), (at_grp(0, 0, 1), blk)]
    greet += [(at_grp(0, dy, 0), blk) for dy in (1, 2, 3)]
    plane = [(0, 0), (0, 1), (0, -1), (0, 2), (0, -2), (1, 1), (1, -1), (1, 2), (1, -2)]
    for dh in range(2):
        greet += [(at_grp(dh, 0, 0), at_blk(dl, dz)) for dl, dz in plane if (dh, dl, dz) != (0, 0, 0)]
    barrier = pltpu.get_barrier_semaphore()
    for dev in greet:
        pl.semaphore_signal(barrier, inc=1, device_id=dev, device_id_type=MESH)
    pl.semaphore_wait(barrier, len(greet))

    down, up, across = (grp, at_blk(0, -1)), (grp, at_blk(0, 1)), (grp, at_blk(1, 0))

    def remote(src, dst, sem, dev):
        return pltpu.make_async_remote_copy(src_ref=src, dst_ref=dst, send_sem=link_send.at[sem],
                                            recv_sem=link_recv.at[sem], device_id=dev, device_id_type=MESH)

    def link(slot, half, i):
        if slot in (P1, M1, Q1):
            span = pl.ds(i * piece, piece)
            src = near.at[P1 - 1, half, span] if slot == Q1 else x.at[span, :, pl.ds(half * 256, 256)]
            return remote(src, near.at[slot - 1, half, span], (slot - 1) * 8 + half * 4 + i,
                          {P1: down, M1: up, Q1: across}[slot])
        if slot == Q2:
            return remote(p2.at[half, i], q2.at[half, i], 42 + half * N_P2 + i, across)
        their_z = z + 1 if slot == M2 else z + 7
        span = pl.ds(lax.rem(their_z + 8 - ORDER[i], 8) * chunk, chunk)
        if slot == M2:
            return remote(near.at[M1 - 1, half, span], m2.at[half, i], 24 + half * N_M2 + i, up)
        return remote(near.at[P1 - 1, half, span], p2.at[half, i], 34 + half * N_P2 + i, down)

    for half in range(2):
        for i in range(4):
            link(P1, half, i).start()
            link(M1, half, i).start()

    def split(a, slot, half, p):
        a = a.reshape(-1, 256)
        top = a.astype(jnp.bfloat16)
        hi[slot, half, p] = top
        lo[slot, half, p] = (a - top.astype(jnp.float32)).astype(jnp.bfloat16)

    def span_at(p):
        return pl.ds(lax.rem(z + 8 - pick(p, ORDER), 8) * chunk, chunk)

    def split_near(slot, half):
        @pl.loop(0, 8)
        def _(p):
            split(near[slot - 1, half, span_at(p)], slot, half, p)

    def split_far(slot, half):
        src, n, keep, base = {M2: (m2, N_M2, M2, 0), P2: (p2, N_P2, P2, 0), Q2: (q2, N_P2, P2, N_P2)}[slot]

        @pl.loop(0, n)
        def _(p):
            split(src[half, p], keep, half, base + p)

    for half in range(2):
        copy = pltpu.make_async_copy(x.at[:, :, pl.ds(half * 256, 256)], own, own_sem)
        copy.start()
        copy.wait()

        @pl.loop(0, 8)
        def _(p):
            split(own[span_at(p)], OWN, half, p)

    def where_is(slot):
        return at_blk(pick(slot, [dl for dl, _ in OFFSET]), pick(slot, [dz for _, dz in OFFSET]))

    def tile_at(tiles, t):
        s, i, u, j = (pick(t, list(field)) for field in zip(*tiles))
        one, two = where_is(s), where_is(u)
        diff = lax.rem(one - two + 16, 16)
        straight = diff <= 8
        pick2 = lambda p, q: jnp.where(straight, p, q)
        return (pick2(s, u), pick2(i, j), pick2(u, s), pick2(j, i), pick2(two, one), pick2(diff, 16 - diff))

    def multiply(batch, group):
        chunks, tiles = BATCHES[batch][group]
        start = FIRST[batch] + sum(len(g) for _, g in BATCHES[batch][:group])

        @pl.loop(0, len(tiles))
        def _(t):
            rows, a, cols, b, _, _ = tile_at(tiles, t)

            def load(buf, slot, half):
                base = 0 if chunks == 8 else jnp.where(slot == Q2, N_P2, 0)
                kept = slot if chunks == 8 else jnp.where(slot == Q2, P2, slot)
                return buf[kept, half, pl.ds(base, chunks)].reshape(-1, 256)

            total = None
            for left, right in ((hi, hi), (hi, lo), (lo, hi)):
                term = lax.dot_general(load(left, rows, a), load(right, cols, b), (((0,), (0,)), ((), ())),
                                       preferred_element_type=jnp.float32)
                total = term if total is None else total + term
            total = total.reshape(4, 2, 32, 256)
            prod[0, start + t] = total[:, 0]
            prod[1, start + t] = total[:, 1]

    def core_copy(batch):
        span = pl.ds(FIRST[batch], COUNT[batch])
        return pltpu.make_async_remote_copy(
            src_ref=prod.at[1 - core, span], dst_ref=core_in.at[span],
            send_sem=core_send.at[batch], recv_sem=core_recv.at[batch],
            device_id=(at_grp(0, 0, 1), blk), device_id_type=MESH)

    def y_copy(batch, dy):
        span = pl.ds(FIRST[batch], COUNT[batch])
        return pltpu.make_async_remote_copy(
            src_ref=prod.at[core, span, lax.rem(y + dy, 4)], dst_ref=y_in.at[dy - 1, span],
            send_sem=y_send.at[batch * 3 + dy - 1], recv_sem=y_recv.at[batch * 3 + dy - 1],
            device_id=(at_grp(0, dy, 0), blk), device_id_type=MESH)

    def core_finish(batch):
        core_copy(batch).wait()

        @pl.loop(FIRST[batch], FIRST[batch] + COUNT[batch])
        def _(q):
            prod[core, q] = prod[core, q] + core_in[q]

        for dy in (1, 2, 3):
            y_copy(batch, dy).start()

    def y_finish(batch):
        for dy in (1, 2, 3):
            y_copy(batch, dy).wait()

        @pl.loop(FIRST[batch], FIRST[batch] + COUNT[batch])
        def _(q):
            prod[core, q, y] = (prod[core, q, y] + y_in[0, q]) + (y_in[1, q] + y_in[2, q])

    def deliver(batch, wait=False):
        start = FIRST[batch]
        for chunks, tiles in BATCHES[batch]:
            @pl.loop(0, len(tiles))
            def _(t, chunks=chunks, tiles=tiles, start=start):
                _, a, _, b, owner, distance = tile_at(tiles, t)
                place = {8: 0, 5: 0, 3: 1, 4: lax.div(z, 4)}[chunks]
                slot = distance + 6 * place
                src, sem = prod.at[core, start + t, y], slot * 4 + h * 2 + b
                mine = jnp.logical_and(a == h, owner == blk)
                if not wait:
                    @pl.when(mine)
                    def _():
                        pltpu.make_async_copy(src, fin.at[slot, h, b], fin_recv.at[sem]).start()

                @pl.when(jnp.logical_not(mine))
                def _():
                    copy = pltpu.make_async_remote_copy(
                        src_ref=src, dst_ref=fin.at[slot, h, b], send_sem=fin_send.at[start + t],
                        recv_sem=fin_recv.at[sem], device_id=(a * 8 + y * 2 + core, owner), device_id_type=MESH)
                    if wait:
                        copy.wait_send()
                    else:
                        copy.start()
            start += len(tiles)

    multiply(0, 0)
    core_copy(0).start()
    for i in range(4):
        link(P1, 0, i).wait_recv()
        link(Q1, 0, i).start()
    for i in range(4):
        link(M1, 0, i).wait_recv()
    for i in range(N_M2):
        if i < N_P2:
            link(P2, 0, i).start()
        link(M2, 0, i).start()
    core_finish(0)
    split_near(P1, 0)
    split_near(M1, 0)
    multiply(1, 0)
    link(P1, 1, 0).wait_recv()
    link(Q1, 1, 0).start()
    for i in range(4):
        link(Q1, 0, i).wait_recv()
    split_near(Q1, 0)
    multiply(1, 1)
    core_copy(1).start()
    link(P1, 1, 1).wait_recv()
    link(Q1, 1, 1).start()
    y_finish(0)
    core_finish(1)
    for i in (2, 3):
        link(P1, 1, i).wait_recv()
        link(Q1, 1, i).start()
    for i in range(4):
        link(M1, 1, i).wait_recv()
    for i in range(N_M2):
        if i < N_P2:
            link(P2, 1, i).start()
        link(M2, 1, i).start()
    split_near(P1, 1)
    split_near(M1, 1)
    multiply(2, 0)
    core_copy(2).start()
    for i in (0, 1):
        link(P2, 0, i).wait_recv()
        link(Q2, 0, i).start()
    for i in range(4):
        link(Q1, 1, i).wait_recv()
    split_near(Q1, 1)
    multiply(3, 0)
    core_copy(3).start()
    y_finish(1)
    for i in (2, 3):
        link(P2, 0, i).wait_recv()
        link(Q2, 0, i).start()
    core_finish(2)
    split_far(P2, 0)
    core_finish(3)
    for i in range(N_M2):
        link(M2, 0, i).wait_recv()
    split_far(M2, 0)
    multiply(4, 0)
    for i in range(N_P2):
        link(Q2, 0, i).wait_recv()
    link(P2, 1, 0).wait_recv()
    link(Q2, 1, 0).start()
    split_far(Q2, 0)
    multiply(4, 1)
    multiply(4, 2)
    core_copy(4).start()
    for i in (1, 2, 3):
        link(P2, 1, i).wait_recv()
        link(Q2, 1, i).start()
    y_finish(2)
    split_far(P2, 1)
    core_finish(4)
    for i in range(N_P2):
        link(Q2, 1, i).wait_recv()
    split_far(Q2, 1)
    multiply(5, 0)
    multiply(5, 1)
    core_copy(5).start()
    y_finish(3)
    for i in range(N_M2):
        link(M2, 1, i).wait_recv()
    for batch in range(4):
        deliver(batch)
    split_far(M2, 1)
    multiply(6, 0)
    multiply(6, 1)
    core_copy(6).start()
    core_finish(5)
    core_finish(6)
    for batch in (4, 5, 6):
        y_finish(batch)
        deliver(batch)

    for d in [0, 1, 2, 6, 7, 8, 3, 4, 5]:
        slots = [d, d + 6] if d in (3, 4, 5) else [d]
        for b in range(2):
            total = None
            for slot in slots:
                for src in range(2):
                    pltpu.make_async_copy(fin.at[slot, src, b], fin.at[slot, src, b],
                                          fin_recv.at[slot * 4 + src * 2 + b]).wait()
                term = fin[slot, 0, b] + fin[slot, 1, b]
                total = term if total is None else total + term
            out[d, :, b * 256:(b + 1) * 256] = total

    for half in range(2):
        for slot, n in ((P1, 4), (M1, 4), (Q1, 4), (M2, N_M2), (P2, N_P2), (Q2, N_P2)):
            for i in range(n):
                link(slot, half, i).wait_send()
    for batch in range(len(BATCHES)):
        deliver(batch, wait=True)


def per_device(factors):
    aux, orbitals, width = factors.shape
    chunk = aux // 8
    dma = pltpu.SemaphoreType.DMA
    n = len(BATCHES)
    out = pl.pallas_call(
        kernel,
        out_shape=jax.ShapeDtypeStruct((9, 32, width), jnp.float32),
        in_specs=[pl.BlockSpec(memory_space=pl.ANY)],
        out_specs=pl.BlockSpec(memory_space=pltpu.VMEM),
        scratch_shapes=[
            pltpu.VMEM((3, 2, aux, orbitals, 256), jnp.float32),
            pltpu.VMEM((2, N_M2, chunk, orbitals, 256), jnp.float32),
            pltpu.VMEM((2, N_P2, chunk, orbitals, 256), jnp.float32),
            pltpu.VMEM((2, N_P2, chunk, orbitals, 256), jnp.float32),
            pltpu.VMEM((aux, orbitals, 256), jnp.float32),
            pltpu.VMEM((6, 2, 8, chunk * orbitals, 256), jnp.bfloat16),
            pltpu.VMEM((6, 2, 8, chunk * orbitals, 256), jnp.bfloat16),
            pltpu.VMEM((2, TILES, 4, 32, 256), jnp.float32),
            pltpu.VMEM((TILES, 4, 32, 256), jnp.float32),
            pltpu.VMEM((3, TILES, 32, 256), jnp.float32),
            pltpu.VMEM((12, 2, 2, 32, 256), jnp.float32),
            dma((50,)), dma((50,)), dma, dma((n,)), dma((n,)), dma((3 * n,)), dma((3 * n,)), dma((TILES,)), dma((48,)),
        ],
        compiler_params=pltpu.CompilerParams(
            collective_id=0, has_side_effects=True, vmem_limit_bytes=62 * 2**20),
        cost_estimate=pl.CostEstimate(flops=6 * 9 * 512 * 512 * aux * orbitals, bytes_accessed=4 * 2**20,
                                      transcendentals=0),
        name="exchange",
    )(factors)
    return out[:, :, None, :]


def solution(mesh):
    return jax.shard_map(
        per_device,
        mesh=mesh,
        in_specs=(P("grp", None, "blk"),),
        out_specs=P(None, "grp", "blk", None),
        check_vma=False,
    )
```

time: 822 us -> 167 us (0.20)
  waiting for transfers between devices: 630 us -> 0 us
  Pallas kernels: 0 us -> 162 us
  matrix products: 113 us -> 0 us
  starting transfers between devices: 38.2 us -> 0 us
  local copies, waits for them, and re-layouts: 27.8 us -> 2.49 us
  between operations: 13.4 us -> 0.01 us
    ppermute x8 -> x0, waiting for transfers between devices: 516 us -> none  [shifted(): return lax.ppermute(block, axis, route)]
    pallas_call x0 -> x1, Pallas kernels: none -> 162 us  [per_device(): pl.pallas_call(kernel, out_shape=jax.ShapeDtypeStruct((9, 32, width), jnp...]
    reduce_scatter x1 -> x0, waiting for transfers between devices: 114 us -> none  [per_device(): result = lax.psum_scatter(result, 'grp', scatter_dimension=1, tiled=True)]
    dot_general x9 -> x0, matrix products: 113 us -> none  [pair_block(): jnp.einsum('pim,pin->mn', visiting, factors, precision=lax.Precision.HIGH...]
    ppermute x8 -> x0, starting transfers between devices: 38.2 us -> none  [shifted(): return lax.ppermute(block, axis, route)]
    while x9 -> x0, local copies, waits for them, and re-layouts: 16.6 us -> none
  transfers between devices with their start and end apart: 9 -> 0, of which waited for: 9 -> 0; matrix products, arithmetic and copies ran while one was open for 0% -> 0% of each run, Pallas kernels for 0% -> 0%
where the time goes in v2:
time: 167 us; the launch traced here: 164 us
  Pallas kernels  162 us (97%)
  local copies, waits for them, and re-layouts  2.49 us (1%)
    pallas_call x1, Pallas kernels, per_device(): pl.pallas_call(kernel, out_shape=jax.ShapeDtypeStruct((9, 32, width), jnp...  162 us

profile of v2, /device:TPU:8, one launch (start us, length us, event | category | flops | bytes accessed | tf_op | source)
XLA Modules:
  0.0 164.1 jit_solution(9912902035913357718)
XLA Ops:
  0.0 161.6 %exchange.1 = f32[9,32,512]{2,1,0:T(8,128)} custom-call(f32[64,24,512]{2,1,0:T(8,128)} %x.1), custom_call_target="tpu_custom_call" | custom-call | flops 21743271936 | bytes 4194304 | tf_op jit(solution)/shard_map/exchange/pallas_call | solution.py:334
  161.7 2.5 %copy.2 = f32[9,32,1,512]{3,2,1,0:T(1,128)} copy(f32[9,32,1,512]{3,1,0,2:T(8,128)} %bitcast.1) | data formatting | bytes 1179648 | tf_op jit(solution)/shard_map/broadcast_in_dim | solution.py:359

commit v3 on v2

--- a/solution.py
+++ b/solution.py
@@ -23,10 +23,12 @@
     [(8, pairs(P1, OWN, A) + pairs(P1, M1, ALL[:1])), (8, pairs(Q1, OWN, A) + pairs(Q1, P1, ALL[:1]) + pairs(Q1, M1, ALL[:1]))],
     [(8, pairs(P1, OWN, B) + pairs(P1, M1, ALL[1:]) + pairs(Q1, P1, ALL[1:2]) + pairs(Q1, M1, ALL[1:2]))],
     [(8, pairs(Q1, OWN, B) + pairs(Q1, P1, B) + pairs(Q1, M1, B))],
-    [(5, pairs(M2, P1, A) + pairs(M2, Q1, A)), (3, pairs(P2, M1, A) + pairs(Q2, M1, A)),
-     (4, pairs(M2, P2, ALL[:1]) + pairs(M2, Q2, ALL[:1]))],
-    [(3, pairs(P2, M1, B) + pairs(Q2, M1, B)), (4, pairs(M2, P2, ALL[1:2]) + pairs(M2, Q2, ALL[1:2]))],
-    [(5, pairs(M2, P1, B) + pairs(M2, Q1, B)), (4, pairs(M2, P2, B) + pairs(M2, Q2, B))],
+    [(5, pairs(M2, P1, A) + pairs(M2, Q1, A)), (3, pairs(P2, M1, A)), (4, pairs(M2, P2, ALL[:1]))],
+    [(3, pairs(Q2, M1, A)), (4, pairs(M2, Q2, ALL[:1]))],
+    [(3, pairs(P2, M1, B)), (4, pairs(M2, P2, ALL[1:2]))],
+    [(3, pairs(Q2, M1, B)), (4, pairs(M2, Q2, ALL[1:2]))],
+    [(4, pairs(M2, P2, B) + pairs(M2, Q2, B))],
+    [(5, pairs(M2, P1, B) + pairs(M2, Q1, B))],
 ]
 FIRST, COUNT = [], []
 for batch in BATCHES:
@@ -106,10 +108,10 @@
         def _(p):
             split(near[slot - 1, half, span_at(p)], slot, half, p)
 
-    def split_far(slot, half):
+    def split_far(slot, half, start=0, stop=None):
         src, n, keep, base = {M2: (m2, N_M2, M2, 0), P2: (p2, N_P2, P2, 0), Q2: (q2, N_P2, P2, N_P2)}[slot]
 
-        @pl.loop(0, n)
+        @pl.loop(start, n if stop is None else stop)
         def _(p):
             split(src[half, p], keep, half, base + p)
 
@@ -162,12 +164,32 @@
             send_sem=core_send.at[batch], recv_sem=core_recv.at[batch],
             device_id=(at_grp(0, 0, 1), blk), device_id_type=MESH)
 
-    def y_copy(batch, dy):
-        span = pl.ds(FIRST[batch], COUNT[batch])
+    def y_copy(batch, leg):
+        first, count = FIRST[batch], COUNT[batch]
+        first, count = [(first, count // 2), (first + count // 2, count - count // 2), (first, count), (first, count)][leg]
+        strip, dy, land = [(2, 1, 0), (2, 3, 0), (1, 1, 1), (3, 3, 2)][leg]
+        span = pl.ds(first, count)
         return pltpu.make_async_remote_copy(
-            src_ref=prod.at[core, span, lax.rem(y + dy, 4)], dst_ref=y_in.at[dy - 1, span],
-            send_sem=y_send.at[batch * 3 + dy - 1], recv_sem=y_recv.at[batch * 3 + dy - 1],
+            src_ref=prod.at[core, span, lax.rem(y + strip, 4)], dst_ref=y_in.at[land, span],
+            send_sem=y_send.at[batch * 4 + leg], recv_sem=y_recv.at[batch * 4 + leg],
             device_id=(at_grp(0, dy, 0), blk), device_id_type=MESH)
+
+    def y_begin(batch):
+        y_copy(batch, 0).start()
+        y_copy(batch, 1).start()
+
+    def y_turn(batch):
+        first, count = FIRST[batch], COUNT[batch]
+        y_copy(batch, 0).wait()
+        y_copy(batch, 1).wait()
+
+        @pl.loop(first, first + count)
+        def _(q):
+            strip = jnp.where(q < first + count // 2, lax.rem(y + 1, 4), lax.rem(y + 3, 4))
+            prod[core, q, strip] = prod[core, q, strip] + y_in[0, q]
+
+        y_copy(batch, 2).start()
+        y_copy(batch, 3).start()
 
     def core_finish(batch):
         core_copy(batch).wait()
@@ -176,16 +198,15 @@
         def _(q):
             prod[core, q] = prod[core, q] + core_in[q]
 
-        for dy in (1, 2, 3):
-            y_copy(batch, dy).start()
+        y_begin(batch)
 
     def y_finish(batch):
-        for dy in (1, 2, 3):
-            y_copy(batch, dy).wait()
+        y_copy(batch, 2).wait()
+        y_copy(batch, 3).wait()
 
         @pl.loop(FIRST[batch], FIRST[batch] + COUNT[batch])
         def _(q):
-            prod[core, q, y] = (prod[core, q, y] + y_in[0, q]) + (y_in[1, q] + y_in[2, q])
+            prod[core, q, y] = prod[core, q, y] + (y_in[1, q] + y_in[2, q])
 
     def deliver(batch, wait=False):
         start = FIRST[batch]
@@ -213,98 +234,123 @@
                         copy.start()
             start += len(tiles)
 
+    def pass_on(slot, then, half, pieces):
+        for i in pieces:
+            link(slot, half, i).wait_recv()
+            link(then, half, i).start()
+
+    def arrive(slot, half, pieces):
+        for i in pieces:
+            link(slot, half, i).wait_recv()
+
+    def second_hops(half):
+        for i in range(N_M2):
+            if i < N_P2:
+                link(P2, half, i).start()
+            link(M2, half, i).start()
+
     multiply(0, 0)
     core_copy(0).start()
-    for i in range(4):
-        link(P1, 0, i).wait_recv()
-        link(Q1, 0, i).start()
-    for i in range(4):
-        link(M1, 0, i).wait_recv()
-    for i in range(N_M2):
-        if i < N_P2:
-            link(P2, 0, i).start()
-        link(M2, 0, i).start()
+    pass_on(P1, Q1, 0, [0])
     core_finish(0)
+    pass_on(P1, Q1, 0, [1])
+    y_turn(0)
+    pass_on(P1, Q1, 0, [2, 3])
+    arrive(M1, 0, range(4))
+    second_hops(0)
     split_near(P1, 0)
     split_near(M1, 0)
     multiply(1, 0)
-    link(P1, 1, 0).wait_recv()
-    link(Q1, 1, 0).start()
-    for i in range(4):
-        link(Q1, 0, i).wait_recv()
+    y_finish(0)
+    pass_on(P1, Q1, 1, [0])
+    arrive(Q1, 0, range(4))
     split_near(Q1, 0)
     multiply(1, 1)
     core_copy(1).start()
-    link(P1, 1, 1).wait_recv()
-    link(Q1, 1, 1).start()
-    y_finish(0)
+    pass_on(P1, Q1, 1, [1])
     core_finish(1)
-    for i in (2, 3):
-        link(P1, 1, i).wait_recv()
-        link(Q1, 1, i).start()
-    for i in range(4):
-        link(M1, 1, i).wait_recv()
-    for i in range(N_M2):
-        if i < N_P2:
-            link(P2, 1, i).start()
-        link(M2, 1, i).start()
+    pass_on(P1, Q1, 1, [2])
+    y_turn(1)
+    pass_on(P1, Q1, 1, [3])
+    arrive(M1, 1, range(4))
+    second_hops(1)
     split_near(P1, 1)
     split_near(M1, 1)
     multiply(2, 0)
     core_copy(2).start()
-    for i in (0, 1):
-        link(P2, 0, i).wait_recv()
-        link(Q2, 0, i).start()
-    for i in range(4):
-        link(Q1, 1, i).wait_recv()
+    y_finish(1)
+    pass_on(P2, Q2, 0, [0, 1])
+    core_finish(2)
+    arrive(Q1, 1, range(4))
     split_near(Q1, 1)
     multiply(3, 0)
     core_copy(3).start()
-    y_finish(1)
-    for i in (2, 3):
-        link(P2, 0, i).wait_recv()
-        link(Q2, 0, i).start()
-    core_finish(2)
+    pass_on(P2, Q2, 0, [2, 3])
+    y_turn(2)
     split_far(P2, 0)
     core_finish(3)
-    for i in range(N_M2):
-        link(M2, 0, i).wait_recv()
+    arrive(M2, 0, range(N_M2))
     split_far(M2, 0)
-    multiply(4, 0)
-    for i in range(N_P2):
-        link(Q2, 0, i).wait_recv()
-    link(P2, 1, 0).wait_recv()
-    link(Q2, 1, 0).start()
+    for group in range(3):
+        multiply(4, group)
+    core_copy(4).start()
+    y_finish(2)
+    y_turn(3)
+    pass_on(P2, Q2, 1, [0])
+    arrive(Q2, 0, range(N_P2))
     split_far(Q2, 0)
-    multiply(4, 1)
-    multiply(4, 2)
-    core_copy(4).start()
-    for i in (1, 2, 3):
-        link(P2, 1, i).wait_recv()
-        link(Q2, 1, i).start()
-    y_finish(2)
+    for group in range(2):
+        multiply(5, group)
+    core_copy(5).start()
+    core_finish(4)
+    pass_on(P2, Q2, 1, [1])
+    y_finish(3)
+    core_finish(5)
+    pass_on(P2, Q2, 1, [2])
+    y_turn(4)
+    pass_on(P2, Q2, 1, [3])
     split_far(P2, 1)
-    core_finish(4)
-    for i in range(N_P2):
-        link(Q2, 1, i).wait_recv()
+    for group in range(2):
+        multiply(6, group)
+    core_copy(6).start()
+    y_turn(5)
+    y_finish(4)
+    core_finish(6)
+    arrive(Q2, 1, range(N_P2))
     split_far(Q2, 1)
-    multiply(5, 0)
-    multiply(5, 1)
-    core_copy(5).start()
-    y_finish(3)
-    for i in range(N_M2):
-        link(M2, 1, i).wait_recv()
-    for batch in range(4):
-        deliver(batch)
-    split_far(M2, 1)
-    multiply(6, 0)
-    multiply(6, 1)
-    core_copy(6).start()
-    core_finish(5)
-    core_finish(6)
-    for batch in (4, 5, 6):
-        y_finish(batch)
-        deliver(batch)
+    for group in range(2):
+        multiply(7, group)
+    core_copy(7).start()
+    y_finish(5)
+    y_turn(6)
+    arrive(M2, 1, range(N_P2))
+    split_far(M2, 1, 0, N_P2)
+    multiply(8, 0)
+    core_copy(8).start()
+    core_finish(7)
+    deliver(0)
+    deliver(1)
+    arrive(M2, 1, range(N_P2, N_M2))
+    split_far(M2, 1, N_P2)
+    multiply(9, 0)
+    core_copy(9).start()
+    core_finish(8)
+    deliver(2)
+    deliver(3)
+    y_turn(7)
+    y_finish(6)
+    deliver(4)
+    core_finish(9)
+    deliver(5)
+    deliver(6)
+    y_turn(8)
+    y_finish(7)
+    deliver(7)
+    y_turn(9)
+    y_finish(8)
+    deliver(8)
+    y_finish(9)
+    deliver(9)
 
     for d in [0, 1, 2, 6, 7, 8, 3, 4, 5]:
         slots = [d, d + 6] if d in (3, 4, 5) else [d]
@@ -348,7 +394,7 @@
             pltpu.VMEM((TILES, 4, 32, 256), jnp.float32),
             pltpu.VMEM((3, TILES, 32, 256), jnp.float32),
             pltpu.VMEM((12, 2, 2, 32, 256), jnp.float32),
-            dma((50,)), dma((50,)), dma, dma((n,)), dma((n,)), dma((3 * n,)), dma((3 * n,)), dma((TILES,)), dma((48,)),
+            dma((50,)), dma((50,)), dma, dma((n,)), dma((n,)), dma((4 * n,)), dma((4 * n,)), dma((TILES,)), dma((48,)),
         ],
         compiler_params=pltpu.CompilerParams(
             collective_id=0, has_side_effects=True, vmem_limit_bytes=62 * 2**20),

time: 167 us -> 159 us (0.952)
  Pallas kernels: 162 us -> 155 us
    pallas_call x1, Pallas kernels: 162 us -> 155 us  [per_device(): pl.pallas_call(kernel, out_shape=jax.ShapeDtypeStruct((9, 32, width), jnp...]
where the time goes in v3:
time: 159 us; the launch traced here: 158 us
  Pallas kernels  155 us (97%)
  local copies, waits for them, and re-layouts  2.49 us (2%)
    pallas_call x1, Pallas kernels, per_device(): pl.pallas_call(kernel, out_shape=jax.ShapeDtypeStruct((9, 32, width), jnp...  155 us

profile of v3, /device:TPU:8, one launch (start us, length us, event | category | flops | bytes accessed | tf_op | source)
XLA Modules:
  0.0 157.6 jit_solution(9813100899103204814)
XLA Ops:
  0.0 155.1 %exchange.1 = f32[9,32,512]{2,1,0:T(8,128)} custom-call(f32[64,24,512]{2,1,0:T(8,128)} %x.1), custom_call_target="tpu_custom_call" | custom-call | flops 21743271936 | bytes 4194304 | tf_op jit(solution)/shard_map/exchange/pallas_call | solution.py:380
  155.1 2.5 %copy.2 = f32[9,32,1,512]{3,2,1,0:T(1,128)} copy(f32[9,32,1,512]{3,1,0,2:T(8,128)} %bitcast.1) | data formatting | bytes 1179648 | tf_op jit(solution)/shard_map/broadcast_in_dim | solution.py:405

commit v4 on v3

--- a/solution.py
+++ b/solution.py
@@ -7,9 +7,10 @@
 
 MESH = pl.DeviceIdType.MESH
 OWN, P1, M1, Q1, M2, P2, Q2 = range(7)
-OFFSET = [(0, 0), (0, 1), (0, -1), (1, 1), (0, -2), (0, 2), (1, 2)]
+OFFSET = [(0, 0), (0, -1), (0, 1), (1, -1), (0, 2), (0, -2), (1, -2)]
 ORDER = [0, 3, 5, 2, 7, 1, 4, 6]
 N_M2, N_P2 = 5, 4
+NEAR = 4
 
 
 def pairs(s, t, halves):
@@ -20,21 +21,22 @@
 A, B = [(0, 0), (0, 1)], [(1, 0), (1, 1)]
 BATCHES = [
     [(8, pairs(OWN, OWN, ALL))],
-    [(8, pairs(P1, OWN, A) + pairs(P1, M1, ALL[:1])), (8, pairs(Q1, OWN, A) + pairs(Q1, P1, ALL[:1]) + pairs(Q1, M1, ALL[:1]))],
-    [(8, pairs(P1, OWN, B) + pairs(P1, M1, ALL[1:]) + pairs(Q1, P1, ALL[1:2]) + pairs(Q1, M1, ALL[1:2]))],
+    [(8, pairs(M1, OWN, A) + pairs(P1, M1, ALL[:1])), (8, pairs(Q1, OWN, A) + pairs(Q1, P1, ALL[:1]) + pairs(Q1, M1, ALL[:1]))],
+    [(8, pairs(M1, OWN, B) + pairs(P1, M1, ALL[1:]) + pairs(Q1, P1, ALL[1:2]) + pairs(Q1, M1, ALL[1:2]))],
     [(8, pairs(Q1, OWN, B) + pairs(Q1, P1, B) + pairs(Q1, M1, B))],
     [(5, pairs(M2, P1, A) + pairs(M2, Q1, A)), (3, pairs(P2, M1, A)), (4, pairs(M2, P2, ALL[:1]))],
     [(3, pairs(Q2, M1, A)), (4, pairs(M2, Q2, ALL[:1]))],
     [(3, pairs(P2, M1, B)), (4, pairs(M2, P2, ALL[1:2]))],
-    [(3, pairs(Q2, M1, B)), (4, pairs(M2, Q2, ALL[1:2]))],
-    [(4, pairs(M2, P2, B) + pairs(M2, Q2, B))],
+    [(4, pairs(M2, P2, B) + pairs(M2, Q2, ALL[2:3]))],
     [(5, pairs(M2, P1, B) + pairs(M2, Q1, B))],
+    [(3, pairs(Q2, M1, B)), (4, pairs(M2, Q2, [(0, 1), (1, 1)]))],
 ]
 FIRST, COUNT = [], []
 for batch in BATCHES:
     FIRST.append(sum(COUNT))
     COUNT.append(sum(len(tiles) for _, tiles in batch))
 TILES = sum(COUNT)
+DIRECT = ()
 
 
 def pick(t, values):
@@ -50,8 +52,9 @@
     grp, blk = lax.axis_index("grp"), lax.axis_index("blk")
     core, y, h = lax.rem(grp, 2), lax.rem(lax.div(grp, 2), 4), lax.div(grp, 8)
     z, row = lax.rem(blk, 8), lax.div(blk, 8)
+    against = lax.rem(8 - z, 8)
     chunk = near.shape[2] // 8
-    piece = near.shape[2] // 4
+    piece = near.shape[2] // NEAR
 
     def at_blk(dl, dz):
         return lax.rem(row + dl, 2) * 8 + lax.rem(z + dz + 8, 8)
@@ -69,7 +72,7 @@
         pl.semaphore_signal(barrier, inc=1, device_id=dev, device_id_type=MESH)
     pl.semaphore_wait(barrier, len(greet))
 
-    down, up, across = (grp, at_blk(0, -1)), (grp, at_blk(0, 1)), (grp, at_blk(1, 0))
+    ahead, back, across = (grp, at_blk(0, 1)), (grp, at_blk(0, -1)), (grp, at_blk(1, 0))
 
     def remote(src, dst, sem, dev):
         return pltpu.make_async_remote_copy(src_ref=src, dst_ref=dst, send_sem=link_send.at[sem],
@@ -79,18 +82,18 @@
         if slot in (P1, M1, Q1):
             span = pl.ds(i * piece, piece)
             src = near.at[P1 - 1, half, span] if slot == Q1 else x.at[span, :, pl.ds(half * 256, 256)]
-            return remote(src, near.at[slot - 1, half, span], (slot - 1) * 8 + half * 4 + i,
-                          {P1: down, M1: up, Q1: across}[slot])
+            return remote(src, near.at[slot - 1, half, span], ((slot - 1) * 2 + half) * NEAR + i,
+                          {P1: ahead, M1: back, Q1: across}[slot])
         if slot == Q2:
-            return remote(p2.at[half, i], q2.at[half, i], 42 + half * N_P2 + i, across)
-        their_z = z + 1 if slot == M2 else z + 7
-        span = pl.ds(lax.rem(their_z + 8 - ORDER[i], 8) * chunk, chunk)
+            return remote(p2.at[half, i], q2.at[half, i], 6 * NEAR + 18 + half * N_P2 + i, across)
+        theirs = against + (1 if slot == M2 else 7)
+        span = pl.ds(lax.rem(theirs + 8 - ORDER[i], 8) * chunk, chunk)
         if slot == M2:
-            return remote(near.at[M1 - 1, half, span], m2.at[half, i], 24 + half * N_M2 + i, up)
-        return remote(near.at[P1 - 1, half, span], p2.at[half, i], 34 + half * N_P2 + i, down)
+            return remote(near.at[M1 - 1, half, span], m2.at[half, i], 6 * NEAR + half * N_M2 + i, back)
+        return remote(near.at[P1 - 1, half, span], p2.at[half, i], 6 * NEAR + 10 + half * N_P2 + i, ahead)
 
     for half in range(2):
-        for i in range(4):
+        for i in range(NEAR):
             link(P1, half, i).start()
             link(M1, half, i).start()
 
@@ -101,7 +104,7 @@
         lo[slot, half, p] = (a - top.astype(jnp.float32)).astype(jnp.bfloat16)
 
     def span_at(p):
-        return pl.ds(lax.rem(z + 8 - pick(p, ORDER), 8) * chunk, chunk)
+        return pl.ds(lax.rem(against + 8 - pick(p, ORDER), 8) * chunk, chunk)
 
     def split_near(slot, half):
         @pl.loop(0, 8)
@@ -133,20 +136,21 @@
         diff = lax.rem(one - two + 16, 16)
         straight = diff <= 8
         pick2 = lambda p, q: jnp.where(straight, p, q)
-        return (pick2(s, u), pick2(i, j), pick2(u, s), pick2(j, i), pick2(two, one), pick2(diff, 16 - diff))
-
-    def multiply(batch, group):
+        return pick2(s, u), pick2(i, j), pick2(u, s), pick2(j, i)
+
+    def multiply(batch, group, skip=0, take=None):
         chunks, tiles = BATCHES[batch][group]
+        take = chunks if take is None else take
         start = FIRST[batch] + sum(len(g) for _, g in BATCHES[batch][:group])
 
         @pl.loop(0, len(tiles))
         def _(t):
-            rows, a, cols, b, _, _ = tile_at(tiles, t)
+            rows, a, cols, b = tile_at(tiles, t)
 
             def load(buf, slot, half):
                 base = 0 if chunks == 8 else jnp.where(slot == Q2, N_P2, 0)
                 kept = slot if chunks == 8 else jnp.where(slot == Q2, P2, slot)
-                return buf[kept, half, pl.ds(base, chunks)].reshape(-1, 256)
+                return buf[kept, half, pl.ds(base + skip, take)].reshape(-1, 256)
 
             total = None
             for left, right in ((hi, hi), (hi, lo), (lo, hi)):
@@ -154,8 +158,9 @@
                                        preferred_element_type=jnp.float32)
                 total = term if total is None else total + term
             total = total.reshape(4, 2, 32, 256)
-            prod[0, start + t] = total[:, 0]
-            prod[1, start + t] = total[:, 1]
+            for k in range(2):
+                strips = total[:, k]
+                prod[k, start + t] = prod[k, start + t] + strips if skip else strips
 
     def core_copy(batch):
         span = pl.ds(FIRST[batch], COUNT[batch])
@@ -166,6 +171,13 @@
 
     def y_copy(batch, leg):
         first, count = FIRST[batch], COUNT[batch]
+        if batch in DIRECT:
+            leg_strip, leg_land = leg + 1, leg
+            span = pl.ds(first, count)
+            return pltpu.make_async_remote_copy(
+                src_ref=prod.at[core, span, lax.rem(y + leg_strip, 4)], dst_ref=y_in.at[leg_land, span],
+                send_sem=y_send.at[batch * 4 + leg], recv_sem=y_recv.at[batch * 4 + leg],
+                device_id=(at_grp(0, leg_strip, 0), blk), device_id_type=MESH)
         first, count = [(first, count // 2), (first + count // 2, count - count // 2), (first, count), (first, count)][leg]
         strip, dy, land = [(2, 1, 0), (2, 3, 0), (1, 1, 1), (3, 3, 2)][leg]
         span = pl.ds(first, count)
@@ -175,11 +187,15 @@
             device_id=(at_grp(0, dy, 0), blk), device_id_type=MESH)
 
     def y_begin(batch):
+        if batch in DIRECT:
+            y_copy(batch, 2).start()
         y_copy(batch, 0).start()
         y_copy(batch, 1).start()
 
     def y_turn(batch):
         first, count = FIRST[batch], COUNT[batch]
+        if batch in DIRECT:
+            return
         y_copy(batch, 0).wait()
         y_copy(batch, 1).wait()
 
@@ -201,38 +217,53 @@
         y_begin(batch)
 
     def y_finish(batch):
-        y_copy(batch, 2).wait()
-        y_copy(batch, 3).wait()
+        for leg in (0, 1, 2) if batch in DIRECT else (2, 3):
+            y_copy(batch, leg).wait()
 
         @pl.loop(FIRST[batch], FIRST[batch] + COUNT[batch])
         def _(q):
-            prod[core, q, y] = prod[core, q, y] + (y_in[1, q] + y_in[2, q])
+            total = prod[core, q, y] + (y_in[1, q] + y_in[2, q])
+            prod[core, q, y] = total + y_in[0, q] if batch in DIRECT else total
+
+    facts = {}
+    for tiles_of in BATCHES:
+        for chunks, tiles in tiles_of:
+            for s, _, u, _ in tiles:
+                if (s, u) not in facts:
+                    one, two = at_blk(*OFFSET[s]), at_blk(*OFFSET[u])
+                    diff = lax.rem(one - two + 16, 16)
+                    straight = diff <= 8
+                    place = {8: 0, 5: 0, 3: 1, 4: lax.div(z, 4)}[chunks]
+                    facts[s, u] = (straight, jnp.where(straight, two, one), jnp.where(straight, diff, 16 - diff) + 6 * place)
 
     def deliver(batch, wait=False):
         start = FIRST[batch]
         for chunks, tiles in BATCHES[batch]:
-            @pl.loop(0, len(tiles))
-            def _(t, chunks=chunks, tiles=tiles, start=start):
-                _, a, _, b, owner, distance = tile_at(tiles, t)
-                place = {8: 0, 5: 0, 3: 1, 4: lax.div(z, 4)}[chunks]
-                slot = distance + 6 * place
-                src, sem = prod.at[core, start + t, y], slot * 4 + h * 2 + b
-                mine = jnp.logical_and(a == h, owner == blk)
-                if not wait:
-                    @pl.when(mine)
+            for pair in dict.fromkeys((s, u) for s, _, u, _ in tiles):
+                halves = [(i, j) for s, i, u, j in tiles if (s, u) == pair]
+                straight, owner, slot = facts[pair]
+
+                @pl.loop(0, len(halves))
+                def _(t, halves=halves, straight=straight, owner=owner, slot=slot, start=start):
+                    i, j = (pick(t, list(side)) for side in zip(*halves))
+                    a, b = jnp.where(straight, i, j), jnp.where(straight, j, i)
+                    src, sem = prod.at[core, start + t, y], slot * 4 + h * 2 + b
+                    mine = jnp.logical_and(a == h, owner == blk)
+                    if not wait:
+                        @pl.when(mine)
+                        def _():
+                            pltpu.make_async_copy(src, fin.at[slot, h, b], fin_recv.at[sem]).start()
+
+                    @pl.when(jnp.logical_not(mine))
                     def _():
-                        pltpu.make_async_copy(src, fin.at[slot, h, b], fin_recv.at[sem]).start()
-
-                @pl.when(jnp.logical_not(mine))
-                def _():
-                    copy = pltpu.make_async_remote_copy(
-                        src_ref=src, dst_ref=fin.at[slot, h, b], send_sem=fin_send.at[start + t],
-                        recv_sem=fin_recv.at[sem], device_id=(a * 8 + y * 2 + core, owner), device_id_type=MESH)
-                    if wait:
-                        copy.wait_send()
-                    else:
-                        copy.start()
-            start += len(tiles)
+                        copy = pltpu.make_async_remote_copy(
+                            src_ref=src, dst_ref=fin.at[slot, h, b], send_sem=fin_send.at[start + t],
+                            recv_sem=fin_recv.at[sem], device_id=(a * 8 + y * 2 + core, owner), device_id_type=MESH)
+                        if wait:
+                            copy.wait_send()
+                        else:
+                            copy.start()
+                start += len(halves)
 
     def pass_on(slot, then, half, pieces):
         for i in pieces:
@@ -251,37 +282,39 @@
 
     multiply(0, 0)
     core_copy(0).start()
-    pass_on(P1, Q1, 0, [0])
+    pass_on(P1, Q1, 0, range(0, NEAR // 4))
     core_finish(0)
-    pass_on(P1, Q1, 0, [1])
+    pass_on(P1, Q1, 0, range(NEAR // 4, NEAR // 2))
     y_turn(0)
-    pass_on(P1, Q1, 0, [2, 3])
-    arrive(M1, 0, range(4))
+    pass_on(P1, Q1, 0, range(NEAR // 2, NEAR))
+    arrive(M1, 0, range(NEAR))
     second_hops(0)
     split_near(P1, 0)
     split_near(M1, 0)
     multiply(1, 0)
     y_finish(0)
-    pass_on(P1, Q1, 1, [0])
-    arrive(Q1, 0, range(4))
+    deliver(0)
+    pass_on(P1, Q1, 1, range(0, NEAR // 4))
+    arrive(Q1, 0, range(NEAR))
     split_near(Q1, 0)
     multiply(1, 1)
     core_copy(1).start()
-    pass_on(P1, Q1, 1, [1])
+    pass_on(P1, Q1, 1, range(NEAR // 4, NEAR // 2))
     core_finish(1)
-    pass_on(P1, Q1, 1, [2])
+    pass_on(P1, Q1, 1, range(NEAR // 2, 3 * NEAR // 4))
     y_turn(1)
-    pass_on(P1, Q1, 1, [3])
-    arrive(M1, 1, range(4))
+    pass_on(P1, Q1, 1, range(3 * NEAR // 4, NEAR))
+    arrive(M1, 1, range(NEAR))
     second_hops(1)
     split_near(P1, 1)
     split_near(M1, 1)
     multiply(2, 0)
     core_copy(2).start()
     y_finish(1)
+    deliver(1)
     pass_on(P2, Q2, 0, [0, 1])
     core_finish(2)
-    arrive(Q1, 1, range(4))
+    arrive(Q1, 1, range(NEAR))
     split_near(Q1, 1)
     multiply(3, 0)
     core_copy(3).start()
@@ -308,47 +341,54 @@
     core_finish(5)
     pass_on(P2, Q2, 1, [2])
     y_turn(4)
+    y_turn(5)
     pass_on(P2, Q2, 1, [3])
     split_far(P2, 1)
     for group in range(2):
         multiply(6, group)
     core_copy(6).start()
-    y_turn(5)
     y_finish(4)
+    arrive(M2, 1, range(N_P2))
+    split_far(M2, 1, 0, N_P2)
+    multiply(7, 0)
+    core_copy(7).start()
     core_finish(6)
+    multiply(8, 0, 0, N_P2)
+    y_finish(5)
+    core_finish(7)
+    y_turn(6)
+    deliver(2)
+    deliver(3)
+    arrive(M2, 1, range(N_P2, N_M2))
+    split_far(M2, 1, N_P2)
+    multiply(8, 0, N_P2, N_M2 - N_P2)
+    core_copy(8).start()
     arrive(Q2, 1, range(N_P2))
     split_far(Q2, 1)
     for group in range(2):
-        multiply(7, group)
-    core_copy(7).start()
-    y_finish(5)
-    y_turn(6)
-    arrive(M2, 1, range(N_P2))
-    split_far(M2, 1, 0, N_P2)
-    multiply(8, 0)
-    core_copy(8).start()
-    core_finish(7)
-    deliver(0)
-    deliver(1)
-    arrive(M2, 1, range(N_P2, N_M2))
-    split_far(M2, 1, N_P2)
-    multiply(9, 0)
+        multiply(9, group)
     core_copy(9).start()
+    deliver(4)
+    y_turn(7)
     core_finish(8)
-    deliver(2)
-    deliver(3)
-    y_turn(7)
+    deliver(5)
+    core_finish(9)
     y_finish(6)
-    deliver(4)
-    core_finish(9)
-    deliver(5)
     deliver(6)
     y_turn(8)
     y_finish(7)
     deliver(7)
     y_turn(9)
+    for half in range(2):
+        for slot, n in ((P1, NEAR), (M1, NEAR), (Q1, NEAR), (M2, N_M2), (P2, N_P2), (Q2, N_P2)):
+            for i in range(n):
+                link(slot, half, i).wait_send()
+    for batch in range(4):
+        deliver(batch, wait=True)
     y_finish(8)
     deliver(8)
+    for batch in range(4, 7):
+        deliver(batch, wait=True)
     y_finish(9)
     deliver(9)
 
@@ -364,11 +404,7 @@
                 total = term if total is None else total + term
             out[d, :, b * 256:(b + 1) * 256] = total
 
-    for half in range(2):
-        for slot, n in ((P1, 4), (M1, 4), (Q1, 4), (M2, N_M2), (P2, N_P2), (Q2, N_P2)):
-            for i in range(n):
-                link(slot, half, i).wait_send()
-    for batch in range(len(BATCHES)):
+    for batch in range(7, len(BATCHES)):
         deliver(batch, wait=True)
 
 
@@ -394,7 +430,7 @@
             pltpu.VMEM((TILES, 4, 32, 256), jnp.float32),
             pltpu.VMEM((3, TILES, 32, 256), jnp.float32),
             pltpu.VMEM((12, 2, 2, 32, 256), jnp.float32),
-            dma((50,)), dma((50,)), dma, dma((n,)), dma((n,)), dma((4 * n,)), dma((4 * n,)), dma((TILES,)), dma((48,)),
+            dma((6 * NEAR + 26,)), dma((6 * NEAR + 26,)), dma, dma((n,)), dma((n,)), dma((4 * n,)), dma((4 * n,)), dma((TILES,)), dma((48,)),
         ],
         compiler_params=pltpu.CompilerParams(
             collective_id=0, has_side_effects=True, vmem_limit_bytes=62 * 2**20),

time: 159 us -> 156 us (0.981)
  Pallas kernels: 155 us -> 153 us
    pallas_call x1, Pallas kernels: 155 us -> 153 us  [per_device(): pl.pallas_call(kernel, out_shape=jax.ShapeDtypeStruct((9, 32, width), jnp...]
where the time goes in v4:
time: 156 us
  Pallas kernels  153 us (98%)
  local copies, waits for them, and re-layouts  2.49 us (2%)
    pallas_call x1, Pallas kernels, per_device(): pl.pallas_call(kernel, out_shape=jax.ShapeDtypeStruct((9, 32, width), jnp...  153 us

profile of v4, /device:TPU:8, one launch (start us, length us, event | category | flops | bytes accessed | tf_op | source)
XLA Modules:
  0.0 155.6 jit_solution(6266476341748614570)
XLA Ops:
  0.0 153.1 %exchange.1 = f32[9,32,512]{2,1,0:T(8,128)} custom-call(f32[64,24,512]{2,1,0:T(8,128)} %x.1), custom_call_target="tpu_custom_call" | custom-call | flops 21743271936 | bytes 4194304 | tf_op jit(solution)/shard_map/exchange/pallas_call | solution.py:416
  153.2 2.5 %copy.2 = f32[9,32,1,512]{3,2,1,0:T(1,128)} copy(f32[9,32,1,512]{3,1,0,2:T(8,128)} %bitcast.1) | data formatting | bytes 1179648 | tf_op jit(solution)/shard_map/broadcast_in_dim | solution.py:441

commit v5 on v4

--- a/solution.py
+++ b/solution.py
@@ -264,6 +264,19 @@
                         else:
                             copy.start()
                 start += len(halves)
+
+    def collect(distances):
+        for d in distances:
+            slots = [d, d + 6] if d in (3, 4, 5) else [d]
+            for b in range(2):
+                total = None
+                for slot in slots:
+                    for src in range(2):
+                        pltpu.make_async_copy(fin.at[slot, src, b], fin.at[slot, src, b],
+                                              fin_recv.at[slot * 4 + src * 2 + b]).wait()
+                    term = fin[slot, 0, b] + fin[slot, 1, b]
+                    total = term if total is None else total + term
+                out[d, :, b * 256:(b + 1) * 256] = total
 
     def pass_on(slot, then, half, pieces):
         for i in pieces:
@@ -387,25 +400,14 @@
         deliver(batch, wait=True)
     y_finish(8)
     deliver(8)
+    collect([0, 1, 2, 6, 7, 8])
     for batch in range(4, 7):
         deliver(batch, wait=True)
     y_finish(9)
     deliver(9)
-
-    for d in [0, 1, 2, 6, 7, 8, 3, 4, 5]:
-        slots = [d, d + 6] if d in (3, 4, 5) else [d]
-        for b in range(2):
-            total = None
-            for slot in slots:
-                for src in range(2):
-                    pltpu.make_async_copy(fin.at[slot, src, b], fin.at[slot, src, b],
-                                          fin_recv.at[slot * 4 + src * 2 + b]).wait()
-                term = fin[slot, 0, b] + fin[slot, 1, b]
-                total = term if total is None else total + term
-            out[d, :, b * 256:(b + 1) * 256] = total
-
     for batch in range(7, len(BATCHES)):
         deliver(batch, wait=True)
+    collect([3, 4, 5])
 
 
 def per_device(factors):

time: 156 us -> 156 us (level)
  no operation moved by 1% of the time
where the time goes in v5:
time: 156 us
  Pallas kernels  153 us (98%)
  local copies, waits for them, and re-layouts  2.49 us (2%)
    pallas_call x1, Pallas kernels, per_device(): pl.pallas_call(kernel, out_shape=jax.ShapeDtypeStruct((9, 32, width), jnp...  153 us

profile of v5, /device:TPU:8, one launch (start us, length us, event | category | flops | bytes accessed | tf_op | source)
XLA Modules:
  0.0 155.5 jit_solution(11052552226653381400)
XLA Ops:
  0.0 153.0 %exchange.1 = f32[9,32,512]{2,1,0:T(8,128)} custom-call(f32[64,24,512]{2,1,0:T(8,128)} %x.1), custom_call_target="tpu_custom_call" | custom-call | flops 21743271936 | bytes 4194304 | tf_op jit(solution)/shard_map/exchange/pallas_call | solution.py:418
  153.0 2.5 %copy.2 = f32[9,32,1,512]{3,2,1,0:T(1,128)} copy(f32[9,32,1,512]{3,1,0,2:T(8,128)} %bitcast.1) | data formatting | bytes 1179648 | tf_op jit(solution)/shard_map/broadcast_in_dim | solution.py:443

commit v6 on v5

--- a/solution.py
+++ b/solution.py
@@ -68,7 +68,7 @@
     for dh in range(2):
         greet += [(at_grp(dh, 0, 0), at_blk(dl, dz)) for dl, dz in plane if (dh, dl, dz) != (0, 0, 0)]
     barrier = pltpu.get_barrier_semaphore()
-    for dev in greet:
+    for dev in reversed(greet):
         pl.semaphore_signal(barrier, inc=1, device_id=dev, device_id_type=MESH)
     pl.semaphore_wait(barrier, len(greet))
 
@@ -276,7 +276,8 @@
                                               fin_recv.at[slot * 4 + src * 2 + b]).wait()
                     term = fin[slot, 0, b] + fin[slot, 1, b]
                     total = term if total is None else total + term
-                out[d, :, b * 256:(b + 1) * 256] = total
+                for c in range(2):
+                    out[pl.ds(d * 128 + b * 2 + c, 32, stride=4), :] = total[:, c * 128:(c + 1) * 128]
 
     def pass_on(slot, then, half, pieces):
         for i in pieces:
@@ -417,7 +418,7 @@
     n = len(BATCHES)
     out = pl.pallas_call(
         kernel,
-        out_shape=jax.ShapeDtypeStruct((9, 32, width), jnp.float32),
+        out_shape=jax.ShapeDtypeStruct((9 * 32 * 4, 128), jnp.float32),
         in_specs=[pl.BlockSpec(memory_space=pl.ANY)],
         out_specs=pl.BlockSpec(memory_space=pltpu.VMEM),
         scratch_shapes=[
@@ -440,7 +441,7 @@
                                       transcendentals=0),
         name="exchange",
     )(factors)
-    return out[:, :, None, :]
+    return out.reshape(9, 32, 1, width)
 
 
 def solution(mesh):

time: 156 us -> 156 us (level)
    broadcast_in_dim x1 -> x0, local copies, waits for them, and re-layouts: 2.49 us -> none  [per_device(): return out[:, :, None, :]]
    unnamed x0 -> x1, local copies, waits for them, and re-layouts: none -> 2.32 us
where the time goes in v6:
time: 156 us; the launch traced here: 155 us
  Pallas kernels  153 us (98%)
  local copies, waits for them, and re-layouts  2.32 us (1%)
    pallas_call x1, Pallas kernels, per_device(): pl.pallas_call(kernel, out_shape=jax.ShapeDtypeStruct((9 * 32 * 4, 128),...  153 us

profile of v6, /device:TPU:8, one launch (start us, length us, event | category | flops | bytes accessed | tf_op | source)
XLA Modules:
  0.0 155.4 jit_solution(3807075225285787365)
XLA Ops:
  0.0 153.1 %exchange.1 = f32[1152,128]{1,0:T(8,128)} custom-call(f32[64,24,512]{2,1,0:T(8,128)} %x.1), custom_call_target="tpu_custom_call" | custom-call | flops 21743271936 | bytes 4194304 | tf_op jit(solution)/shard_map/exchange/pallas_call | solution.py:419
  153.1 2.3 %copy.4 = f32[9,32,1,512]{3,2,1,0:T(1,128)} copy(f32[9,32,1,512]{3,2,1,0:T(1,128)} %bitcast.1) | data formatting | bytes 1179648
